TPU v7x, 32 devices: a whole 2x2x4 slice. The times are simulated.
32 devices in a mesh: branch: 2 (over core), prow: 8 (over z, x), pcol: 2 (over y).
Axes of the slice: x: 2, y: 2, z: 4, core: 2. Of those that a mesh axis runs over, the one named last changes fastest.
Arguments:
- pair_rep: float32 [128, 128, 128], P(('branch', 'prow'), 'pcol'), may hold values from -6 to 6
- alignment: float32 [8, 128, 256], P('pcol', ('branch', 'prow')), may hold values from -6 to 6
- residue_mask: int32 [128], replicated, may hold values 0 or 1
- row_mask: int32 [8, 128], P('pcol', ('branch', 'prow')), may hold values 0 or 1
- attention_in: float32 [256, 1024], replicated, may hold values from -0.375 to 0.375
- pair_bias_w: float32 [128, 8], replicated, may hold values from -40 to 40
- attention_out: float32 [256, 256], replicated, may hold values from -0.375 to 0.375
- outer_in: float32 [256, 64], replicated, may hold values from -0.375 to 0.375
- outer_out: float32 [1024, 128], replicated, may hold values from -0.1875 to 0.1875
- triangle_in: float32 [128, 512], replicated, may hold values from -0.5 to 0.5
- triangle_gate: float32 [128, 128], replicated, may hold values from -0.5 to 0.5
- triangle_out: float32 [128, 128], replicated, may hold values from -0.5 to 0.5
- transit_in: float32 [128, 512], replicated, may hold values from -0.5 to 0.5
- transit_out: float32 [512, 128], replicated, may hold values from -0.25 to 0.25
Outputs:
- new_alignment: float32 [8, 128, 256], P('pcol', ('branch', 'prow'))
- new_pair: float32 [128, 128, 128], P(('branch', 'prow'), 'pcol')
All inputs are finite; a program needn't handle non-finite values. No bound on the sum of `row_mask` on one device may be relied on, other than what follows from the above.
Results may differ from a plain program's by a relative error of at most 0.0003.
Values sent between devices are 32-bit elements; how exact they have to be, the bound alone decides.
A program may use at most 64 MiB of HBM per device.

v0:
```python
import jax
import jax.numpy as jnp
from jax import lax
from jax.sharding import PartitionSpec as P

highest = lax.Precision.HIGHEST
epsilon = 1e-05


def layer_norm(values):
    center = values - jnp.mean(values, axis=-1, keepdims=True)
    spread = jnp.mean(center * center, axis=-1, keepdims=True)
    return center * lax.rsqrt(spread + epsilon)


def matmul(left_side, right_side):
    return jnp.dot(left_side, right_side, precision=highest, preferred_element_type=jnp.float32)


def outer_block(left_rows, right_cols, outer_out):
    product = jnp.einsum("sip,sjq->ijpq", left_rows, right_cols, precision=highest)
    row_total, col_total, left_width, right_width = product.shape
    return matmul(product.reshape(row_total, col_total, left_width * right_width), outer_out)


def shards(
    pair_rep,
    alignment,
    residue_mask,
    row_mask,
    attention_in,
    pair_bias_w,
    attention_out,
    outer_in,
    outer_out,
    triangle_in,
    triangle_gate,
    triangle_out,
    transit_in,
    transit_out,
):
    row_count, col_count, _ = pair_rep.shape
    seq_count = alignment.shape[0]
    head_count = pair_bias_w.shape[1]
    att_width = attention_out.shape[0]
    head_depth = att_width // head_count
    outer_width = outer_in.shape[1] // 2
    inner_width = triangle_out.shape[0]
    row_start = lax.axis_index(("branch", "prow")) * row_count
    col_start = lax.axis_index("pcol") * col_count
    pair_norm = layer_norm(pair_rep)
    bias_tile = jnp.einsum("ijc,ch->hij", pair_norm, pair_bias_w, precision=highest)
    bias_rows = lax.all_gather(bias_tile, "pcol", axis=2, tiled=True)
    normed = layer_norm(alignment)
    mask_float = row_mask.astype(jnp.float32)
    key_bias = 1000000000.0 * (mask_float - 1.0)
    queries = matmul(normed, attention_in[:, :att_width]) * head_depth ** (-0.5)
    queries = queries.reshape(seq_count, row_count, head_count, head_depth)
    gate_logits = matmul(normed, attention_in[:, 3 * att_width :])
    key_value_w = attention_in[:, att_width : 3 * att_width]
    key_value_local = matmul(normed, key_value_w)
    widen = lambda sent_block: sent_block
    running_max = jnp.full((seq_count, head_count, row_count), -1e30, jnp.float32)
    make_sent_block = lax.all_gather(key_value_local, ("branch", "prow"), axis=1, tiled=True)
    block_bias = lax.all_gather(key_bias, ("branch", "prow"), axis=1, tiled=True)
    key_value = widen(make_sent_block)
    key_count = block_bias.shape[1]
    key_block = key_value[..., :att_width].reshape(seq_count, key_count, head_count, head_depth)
    value_block = key_value[..., att_width:].reshape(seq_count, key_count, head_count, head_depth)
    scores = jnp.einsum("sihd,sjhd->shij", queries, key_block, precision=highest)
    scores = scores + bias_rows[None] + block_bias[:, None, None, :]
    block_max = jnp.maximum(running_max, jnp.max(scores, axis=-1))
    weights = jnp.exp(scores - block_max[..., None])
    running_sum = jnp.sum(weights, axis=-1)
    accumulated = jnp.einsum("shij,sjhd->shid", weights, value_block, precision=highest)
    final_state = (block_max, running_sum, accumulated)
    _, running_sum, accumulated = final_state
    mixed = accumulated / running_sum[..., None]
    mixed = jnp.transpose(mixed, (0, 2, 1, 3)).reshape(seq_count, row_count, att_width)
    new_alignment = alignment + matmul(mixed * jax.nn.sigmoid(gate_logits), attention_out)
    factors = matmul(layer_norm(new_alignment), outer_in) * mask_float[..., None]
    left_outer = factors[..., :outer_width]
    right_outer = factors[..., outer_width:]
    right_all, mask_all = (
        lax.all_gather(right_outer, ("branch", "prow"), axis=1, tiled=True),
        lax.all_gather(mask_float, ("branch", "prow"), axis=1, tiled=True),
    )
    left_full, left_mask = (
        lax.all_gather(left_outer, "pcol", axis=0, tiled=True),
        lax.all_gather(mask_float, "pcol", axis=0, tiled=True),
    )
    right_tile, mask_tile = (
        lax.all_to_all(right_all, "pcol", split_axis=1, concat_axis=0, tiled=True),
        lax.all_to_all(mask_all, "pcol", split_axis=1, concat_axis=0, tiled=True),
    )
    outer_sum = outer_block(left_full, right_tile, outer_out)
    count_sum = jnp.einsum("si,sj->ij", left_mask, mask_tile, precision=highest)
    outer_mean = outer_sum / (1.0 + count_sum)[..., None]
    pair_one = pair_rep + outer_mean
    tri_norm = layer_norm(pair_one)
    res_float = residue_mask.astype(jnp.float32)
    row_valid = lax.dynamic_slice_in_dim(res_float, row_start, row_count)
    col_valid = lax.dynamic_slice_in_dim(res_float, col_start, col_count)
    pair_valid = (row_valid[:, None] * col_valid[None, :])[..., None]
    edges = matmul(tri_norm, triangle_in)
    left_edge = (
        jax.nn.sigmoid(edges[..., :inner_width])
        * edges[..., inner_width : 2 * inner_width]
        * pair_valid
    )
    right_edge = (
        jax.nn.sigmoid(edges[..., 2 * inner_width : 3 * inner_width])
        * edges[..., 3 * inner_width :]
        * pair_valid
    )
    cross_part = jnp.einsum(
        "ikc,jkc->ijc",
        left_edge,
        lax.all_gather(right_edge, ("branch", "prow"), axis=0, tiled=True),
        precision=highest,
    )
    crossed = lax.psum_scatter(cross_part, "pcol", scatter_dimension=1, tiled=True)
    triangle = matmul(layer_norm(crossed), triangle_out) * jax.nn.sigmoid(
        matmul(tri_norm, triangle_gate)
    )
    pair_mid = pair_one + triangle
    hidden_units = jax.nn.relu(matmul(layer_norm(pair_mid), transit_in))
    new_pair = pair_mid + matmul(hidden_units, transit_out)
    return (new_alignment, new_pair)


def solution(mesh):
    return jax.shard_map(
        shards,
        mesh=mesh,
        in_specs=(
            P(("branch", "prow"), "pcol", None),
            P("pcol", ("branch", "prow"), None),
            P(),
            P("pcol", ("branch", "prow")),
            P(),
            P(),
            P(),
            P(),
            P(),
            P(),
            P(),
            P(),
            P(),
            P(),
        ),
        out_specs=(P("pcol", ("branch", "prow"), None), P(("branch", "prow"), "pcol", None)),
        check_vma=False,
    )
```

profile of v0, /device:TPU:0, one launch (start us, length us, event | category | flops | bytes accessed | tf_op | source)
XLA Modules:
  0.0 266.0 jit_solution(14166911760422959844)
XLA Ops:
  7.2 0.9 reduce_sum.117
  8.1 0.9 multiply_reduce_fusion.5
  9.0 2.1 fusion.12
  11.9 34.3 %all-gather.2 = f32[16,8,4]{1,2,0:T(4,128)S(1)} all-gather(f32[1,8,4]{1,2,0:T(4,128)S(1)} %get-tuple-element.8), channel_id=1, replica_groups=mesh['branch'=2,'prow'=8,'pcol'=2] {'branch','prow'}, dimensions={0}, use_global_device_ids=true | all-gather | bytes 2176 | tf_op jit(solution)/shard_map/all_gather | solution.py:86
  47.0 3.2 %all-to-all-start.1 = ((f32[2,1,256]{2,1,0:T(1,128)}), f32[2,1,256]{2,1,0:T(1,128)S(1)}, u32[]{:S(2)}, u32[]{:S(2)}) async-start(f32[2,1,256]{2,1,0:T(1,128)} %reshape.156), calls=%async_computation.1 | async-start | bytes 4096 | tf_op jit(solution)/shard_map/all_to_all | solution.py:94
  50.2 1.2 convolution_multiply_fusion.1
  51.6 1.1 reduce_sum.119
  52.7 1.2 multiply_reduce_fusion.3
  53.9 1.8 convolution_bitcast_fusion.3
  55.9 9.5 %all_gather.25 = f32[8,8,128]{1,0,2:T(8,128)S(1)} all-gather(f32[8,8,64]{1,0,2:T(8,128)S(1)} %copy.86), channel_id=1, replica_groups=mesh['branch'=2,'prow'=8,'pcol'=2] {'pcol'}, dimensions={2}, use_global_device_ids=true | all-gather | bytes 49152 | tf_op jit(solution)/shard_map/all_gather | solution.py:53
  67.1 28.6 %all-gather = f32[16,8,4]{1,2,0:T(4,128)S(1)} all-gather(f32[1,8,4]{1,2,0:T(4,128)S(1)} %multiply_bitcast_fusion), channel_id=1, replica_groups=mesh['branch'=2,'prow'=8,'pcol'=2] {'branch','prow'}, dimensions={0}, use_global_device_ids=true | all-gather | bytes 2176 | tf_op jit(solution)/shard_map/all_gather | solution.py:65
  95.8 4.3 %all-gather.1 = f32[2,4,8]{2,1,0:T(4,128)S(1)} all-gather(f32[1,4,8]{2,1,0:T(4,128)S(1)} %get-tuple-element.9), channel_id=1, replica_groups=mesh['branch'=2,'prow'=8,'pcol'=2] {'pcol'}, dimensions={0}, use_global_device_ids=true | all-gather | bytes 384 | tf_op jit(solution)/shard_map/all_gather | solution.py:90
  101.5 1.3 fusion.68
  104.1 1.0 fusion.5
  105.2 1.2 fusion.10
  107.3 32.1 %all_gather.27 = f32[4,128,32]{2,1,0:T(8,128)S(1)} all-gather(f32[4,8,32]{2,1,0:T(8,128)S(1)} %get-tuple-element.7), channel_id=1, replica_groups=mesh['branch'=2,'prow'=8,'pcol'=2] {'branch','prow'}, dimensions={1}, use_global_device_ids=true | all-gather | bytes 69632 | tf_op jit(solution)/shard_map/all_gather | solution.py:85
  140.5 3.3 %all-to-all-start = ((f32[2,1,8192]{2,1,0:T(1,128)}), f32[2,1,8192]{2,1,0:T(1,128)S(1)}, u32[]{:S(2)}, u32[]{:S(2)}) async-start(f32[2,1,8192]{2,1,0:T(1,128)} %reshape.154), calls=%async_computation | async-start | bytes 131072 | tf_op jit(solution)/shard_map/all_to_all | solution.py:93
  144.0 4.6 %all_gather.28 = f32[8,8,32]{2,1,0:T(8,128)S(1)} all-gather(f32[4,8,32]{2,1,0:T(8,128)S(1)} %get-tuple-element.6), channel_id=1, replica_groups=mesh['branch'=2,'prow'=8,'pcol'=2] {'pcol'}, dimensions={0}, use_global_device_ids=true | all-gather | bytes 12288 | tf_op jit(solution)/shard_map/all_gather | solution.py:89
  149.8 3.5 %convolution_bitcast_fusion = f32[8,64,32,32]{1,2,0,3:T(8,128)S(1)} fusion(f32[8,64,32,1]{1,0,3,2:T(8,128)S(1)} %bitcast.112, f32[8,8,32]{2,1,0:T(8,128)S(1)} %all_gather.28), kind=kOutput, calls=%fused_computation | convolution fusion | flops 50331648 | bytes 2170880 | tf_op jit(solution)/shard_map/sip,sjq->ijpq/dot_general | solution.py:21
  153.3 2.4 copy.94
  155.8 6.8 %fusion.72 = (f32[8,64]{1,0:T(8,128)S(1)}, f32[8,64,128]{2,1,0:T(8,128)S(1)}) fusion(f32[8,64,128]{2,1,0:T(8,128)S(1)} %copy-done.1, f32[8,64]{1,0:T(8,128)S(1)} %convolution_add_fusion.3, f32[8,64,1024]{1,2,0:T(8,128)S(1)} %bitcast.107, f32[1024,128]{1,0:T(8,128)S(1)} %copy-done), kind=kOutput, calls=%fused_computation.117 | convolution fusion | flops 805502464 | bytes 3149824 | tf_op jit(solution)/shard_map/dot_general | solution.py:17
  162.8 1.3 fusion.25
  165.3 48.1 %all-gather.8.cloned.1.call-done = f32[128,64,128]{2,1,0:T(8,128)} async-done(((f32[8,64,128]{2,1,0:T(8,128)}), f32[128,64,128]{2,1,0:T(8,128)}) %all-gather.8.cloned.1.call-update) | async-done | bytes 4194320 | tf_op jit(solution)/shard_map/all_gather | solution.py:119
  213.4 9.1 %copy.98 = f32[128,64,128]{1,0,2:T(8,128)} copy(f32[128,64,128]{2,1,0:T(8,128)} %all-gather.8.cloned.1.call-done) | data formatting | bytes 8388608 | tf_op jit(solution)/shard_map/all_gather | solution.py:119
  222.6 15.4 %convolution_bitcast_fusion.1 = f32[8,128,128]{1,0,2:T(8,128)S(1)} fusion(f32[128,64,128]{1,0,2:T(8,128)} %copy.98, f32[8,64,128]{1,0,2:T(8,128)S(1)} %copy.99), kind=kOutput, calls=%fused_computation.2 | convolution fusion | flops 100663296 | bytes 4980736 | tf_op jit(solution)/shard_map/ikc,jkc->ijc/dot_general | solution.py:116
  238.0 1.0 copy.100
  239.5 12.7 %reduce-scatter.2.cloned.1.call-done = f32[8,64,128]{2,0,1:T(8,128)} async-done(((f32[8,128,128]{2,0,1:T(8,128)}), f32[8,64,128]{2,0,1:T(8,128)}) %reduce-scatter.2.cloned.1.call-update) | async-done | bytes 262160 | tf_op jit(solution)/shard_map/reduce_scatter | solution.py:122
  252.2 1.1 reduce_sum.126
  253.5 1.2 multiply_reduce_fusion.1
  254.8 1.2 subtract_multiply_fusion
  256.8 1.0 convolution_maximum_fusion
  257.8 1.7 convolution_add_fusion
  (89 shorter events, 12.7 us)
Async XLA Ops:
  7.2 148.6 %copy-start = (f32[1024,128]{1,0:T(8,128)S(1)}, f32[1024,128]{1,0:T(8,128)}, u32[]{:S(2)}) copy-start(f32[1024,128]{1,0:T(8,128)} %param.22) | copy-start | bytes 1572868
  7.2 94.4 %all-gather.6.cloned.1.call-start = ((), (), s32[]{:S(2)}) async-start(), calls=%async_computation.3 | async-start | bytes 1114112 | tf_op jit(solution)/shard_map/all_gather | solution.py:64
  47.0 53.1 %all-to-all-start.1 = ((f32[2,1,256]{2,1,0:T(1,128)}), f32[2,1,256]{2,1,0:T(1,128)S(1)}, u32[]{:S(2)}, u32[]{:S(2)}) async-start(f32[2,1,256]{2,1,0:T(1,128)} %reshape.156), calls=%async_computation.1 | async-start | bytes 4096 | tf_op jit(solution)/shard_map/all_to_all | solution.py:94
  55.7 49.5 %copy-start.2 = (f32[4,8,256]{2,1,0:T(8,128)S(1)}, f32[4,8,256]{2,1,0:T(8,128)}, u32[]{:S(2)}) copy-start(f32[4,8,256]{2,1,0:T(8,128)} %param.15) | copy-start | bytes 98308
  55.9 50.6 %copy-start.4 = (f32[256,256]{1,0:T(8,128)S(1)}, f32[256,256]{1,0:T(8,128)}, u32[]{:S(2)}) copy-start(f32[256,256]{1,0:T(8,128)} %param.20) | copy-start | bytes 786436
  65.4 41.6 %copy-start.9 = (f32[256,64]{0,1:T(8,128)S(1)}, f32[256,64]{0,1:T(8,128)}, u32[]{:S(2)}) copy-start(f32[256,64]{0,1:T(8,128)} %param.21) | copy-start | bytes 196612
  106.8 48.9 %copy-start.7 = (f32[4,8,256]{2,1,0:T(8,128)}, f32[4,8,256]{2,1,0:T(8,128)S(1)}, u32[]{:S(2)}) copy-start(f32[4,8,256]{2,1,0:T(8,128)S(1)} %get-tuple-element.14) | copy-start | bytes 98308
  140.5 8.1 %all-to-all-start = ((f32[2,1,8192]{2,1,0:T(1,128)}), f32[2,1,8192]{2,1,0:T(1,128)S(1)}, u32[]{:S(2)}, u32[]{:S(2)}) async-start(f32[2,1,8192]{2,1,0:T(1,128)} %reshape.154), calls=%async_computation | async-start | bytes 131072 | tf_op jit(solution)/shard_map/all_to_all | solution.py:93
  143.8 69.7 %all-gather.8.cloned.1.call-start = ((), (), s32[]{:S(2)}) async-start(), calls=%async_computation.4 | async-start | bytes 4456448 | tf_op jit(solution)/shard_map/all_gather | solution.py:119
  153.3 2.4 copy-start.1
  155.7 7.1 %copy-start.5 = (f32[128,512]{1,0:T(8,128)S(1)}, f32[128,512]{1,0:T(8,128)}, u32[]{:S(2)}) copy-start(f32[128,512]{1,0:T(8,128)} %param.23) | copy-start | bytes 786436
  165.0 87.2 %reduce-scatter.2.cloned.1.call-start = ((), (), s32[]{:S(2)}) async-start(), calls=%async_computation.5 | async-start | bytes 786432 | tf_op jit(solution)/shard_map/reduce_scatter | solution.py:122
  222.6 16.5 %copy-start.10 = (f32[128,128]{1,0:T(8,128)S(1)}, f32[128,128]{1,0:T(8,128)}, u32[]{:S(2)}) copy-start(f32[128,128]{1,0:T(8,128)} %param.24) | copy-start | bytes 196612
  237.9 18.0 %copy-start.8 = (f32[128,128]{1,0:T(8,128)S(1)}, f32[128,128]{1,0:T(8,128)}, u32[]{:S(2)}) copy-start(f32[128,128]{1,0:T(8,128)} %param.25) | copy-start | bytes 196612
  237.9 18.8 %copy-start.6 = (f32[128,512]{1,0:T(8,128)S(1)}, f32[128,512]{1,0:T(8,128)}, u32[]{:S(2)}) copy-start(f32[128,512]{1,0:T(8,128)} %param.26) | copy-start | bytes 786436
  237.9 19.8 %copy-start.3 = (f32[512,128]{1,0:T(8,128)S(1)}, f32[512,128]{1,0:T(8,128)}, u32[]{:S(2)}) copy-start(f32[512,128]{1,0:T(8,128)} %param.27) | copy-start | bytes 786436
Sparse Core Ops, SparseCore 0:
  11.3 40.6 all-gather.5
  165.1 48.2 all-gather.7
  239.1 13.0 reduce-scatter.1
where the time goes:
time: 267 us; the launch traced here: 266 us
  blocking collectives  113 us (42%)
  waiting for transfers between devices  60.9 us (23%)
  matrix products  39.3 us (15%)
  local copies, waits for them, and re-layouts  18.5 us (7%)
  between operations  14.2 us (5%)
  other arithmetic  13.1 us (5%)
  starting transfers between devices  6.64 us (2%)
    all_gather x1, waiting for transfers between devices, shards(): lax.all_gather(right_edge, ('branch', 'prow'), axis=0, tiled=True)  48.1 us
    all_gather x1, blocking collectives, shards(): lax.all_gather(mask_float, ('branch', 'prow'), axis=1, tiled=True)  34.3 us
    all_gather x1, blocking collectives, shards(): lax.all_gather(right_outer, ('branch', 'prow'), axis=1, tiled=True)  32.1 us
    all_gather x1, blocking collectives, shards(): lax.all_gather(key_bias, ('branch', 'prow'), axis=1, tiled=True)  28.6 us
    dot_general x11, matrix products, matmul(): jnp.dot(left_side, right_side, precision=highest, preferred_element_type=...  16.8 us
    dot_general x1, matrix products, shards(): jnp.einsum('ikc,jkc->ijc', left_edge, lax.all_gather(right_edge, ('branch...  15.4 us
    reduce_scatter x1, waiting for transfers between devices, shards(): lax.psum_scatter(cross_part, 'pcol', scatter_dimension=1, tiled=True)  12.7 us
    all_gather x1, blocking collectives, shards(): bias_rows = lax.all_gather(bias_tile, 'pcol', axis=2, tiled=True)  9.47 us
  transfers between devices with their start and end apart: 5, of which 2 were waited for; matrix products, arithmetic and copies ran while one was open for 4% of the time, Pallas kernels for 0%

commit v1 on v0

--- a/solution.py
+++ b/solution.py
@@ -1,7 +1,16 @@
+import functools
+
 import jax
 import jax.numpy as jnp
+import numpy as np
 from jax import lax
+from jax.experimental import pallas as pl
+from jax.experimental.pallas import tpu as pltpu
 from jax.sharding import PartitionSpec as P
+
+MESH = pl.DeviceIdType.MESH
+NN = (((1,), (0,)), ((), ()))
+NT = (((1,), (1,)), ((), ()))
 
 highest = lax.Precision.HIGHEST
 epsilon = 1e-05
@@ -129,9 +138,470 @@
     return (new_alignment, new_pair)
 
 
+def split(values):
+    high = values.astype(jnp.bfloat16)
+    return high, (values - high.astype(jnp.float32)).astype(jnp.bfloat16)
+
+
+def dot(a, b, dims=NN):
+    return lax.dot_general(a, b, dims, preferred_element_type=jnp.float32)
+
+
+def dot_split(a, b, dims=NN):
+    return dot(a[0], b[0], dims) + (dot(a[0], b[1], dims) + dot(a[1], b[0], dims))
+
+
+def mm(a, b, dims=NN):
+    return dot_split(split(a), split(b), dims)
+
+
+def mm_high(a, b, dims=NN):
+    return lax.dot_general(a, b, dims, precision=highest, preferred_element_type=jnp.float32)
+
+
+def sigmoid(v):
+    return 1.0 / (1.0 + jnp.exp(-v))
+
+
+def pick(matrix, pair, dims=NN):
+    return tuple(dot(matrix, part, dims).astype(jnp.bfloat16) for part in pair)
+
+
+def pick_right(pair, matrix):
+    return tuple(dot(part, matrix).astype(jnp.bfloat16) for part in pair)
+
+
+def block_kernel(
+    sizes,
+    pair_ref, ali_ref, res_ref, row_ref, ain_ref, pbw_ref, aout_ref, oin_ref, oout_ref,
+    tin_ref, tgate_ref, tout_ref, xin_ref, xout_ref,
+    perm_outer_ref, perm_gate_ref, perm_value_ref, perm_row_ref, pos_ref,
+    nali_ref, npair_ref,
+    qsend, qrecv, bsend, brecv, msend, mrecv, frs, frr, fls, flr, es, er, cs, cr,
+    lsc, tsc, p1, xs, send_sem, recv_sem,
+):
+    nb, np_, nc = sizes
+    nr = nb * np_
+    nd = nr * nc
+    rb, cb, cz = pair_ref.shape
+    sb, _, cm = ali_ref.shape
+    seq = sb * nc
+    res = rb * nr
+    heads = pbw_ref.shape[1]
+    att = aout_ref.shape[0]
+    depth = att // heads
+    groups = nr // sb
+    hpg = heads // groups
+    gw = hpg * depth
+    ow = oin_ref.shape[1] // 2
+    tri = tout_ref.shape[0]
+    cpd = tri // nd
+    per = nr // nc
+    pos = rb * cb
+    nib = pos // 128
+    f32 = jnp.float32
+
+    r_me = lax.axis_index("branch") * np_ + lax.axis_index("prow")
+    p_me = lax.axis_index("pcol")
+    me = r_me * nc + p_me
+
+    def where(r, p):
+        return {"branch": r // np_, "prow": lax.rem(r, np_), "pcol": p}
+
+    def al(v, m):
+        return pl.multiple_of(v, m)
+
+    def copy(phase, src, dst, tag, origin, r, p):
+        return pltpu.make_async_remote_copy(
+            src_ref=src, dst_ref=dst, send_sem=send_sem.at[phase, tag],
+            recv_sem=recv_sem.at[phase, origin], device_id=where(r, p), device_id_type=MESH,
+        )
+
+    barrier = pltpu.get_barrier_semaphore()
+
+    @pl.loop(1, nd)
+    def _(k):
+        t = lax.rem(me + k, nd)
+        pl.semaphore_signal(barrier, inc=1, device_id=where(t // nc, lax.rem(t, nc)), device_id_type=MESH)
+
+    pair = pair_ref[...].reshape(pos, cz)
+    pair_norm = layer_norm(pair)
+    for i in range(rb):
+        bsend[:, i, :] = mm_high(pbw_ref[...].T, pair_norm[i * cb : (i + 1) * cb], NT)
+
+    pl.semaphore_wait(barrier, nd - 1)
+
+    def b_copy(r, p, origin_r, origin_p):
+        group = lax.rem(r, groups)
+        return copy(
+            1, bsend.at[pl.ds(group * hpg, hpg)],
+            brecv.at[origin_p, :, pl.ds(al(origin_r * rb, rb), rb), :],
+            r * nc + p, origin_r * nc + origin_p, r, p,
+        )
+
+    @pl.loop(1, nd)
+    def _(k):
+        t = lax.rem(me + k, nd)
+        b_copy(t // nc, lax.rem(t, nc), r_me, p_me).start()
+
+    brecv[p_me, :, pl.ds(al(r_me * rb, rb), rb), :] = bsend[pl.ds(lax.rem(r_me, groups) * hpg, hpg)]
+
+    ali = ali_ref[...].reshape(sb * rb, cm)
+    projected = mm_high(layer_norm(ali), ain_ref[...])
+    gate = sigmoid(projected[:, 3 * att :])
+    mask = row_ref[...].astype(f32)
+    eye = (
+        lax.broadcasted_iota(jnp.int32, (rb, rb), 0) == lax.broadcasted_iota(jnp.int32, (rb, rb), 1)
+    ).astype(f32)
+    mask_cols = [jnp.sum(eye * mask[s : s + 1, :], axis=1, keepdims=True) for s in range(sb)]
+    for s in range(sb):
+        rows = projected[s * rb : (s + 1) * rb]
+        for g in range(groups):
+            for n in range(3):
+                qsend[s * groups + g, :, n * gw : (n + 1) * gw] = rows[
+                    :, n * att + g * gw : n * att + (g + 1) * gw
+                ]
+            qsend[s * groups + g, :, 3 * gw :] = jnp.broadcast_to(mask_cols[s], (rb, gw))
+
+    def q_copy(r, origin_r):
+        return copy(
+            0, qsend.at[r], qrecv.at[pl.ds(al(origin_r * rb, rb), rb), :], r, origin_r, r, p_me
+        )
+
+    @pl.loop(1, nr)
+    def _(k):
+        q_copy(lax.rem(r_me + k, nr), r_me).start()
+
+    qrecv[pl.ds(al(r_me * rb, rb), rb), :] = qsend[r_me]
+
+    tin = split(tin_ref[...])
+    w_gate = pick(perm_gate_ref[...], tin, NT)
+    w_value = pick(perm_value_ref[...], tin, NT)
+    res_rows = jnp.broadcast_to(res_ref[...].astype(f32), (8, res)).astype(jnp.bfloat16)
+    index = lax.broadcasted_iota(jnp.int32, (res, pos), 0)
+    row_pick = (index == pos_ref[0:1, :] + r_me * rb).astype(jnp.bfloat16)
+    col_pick = (index == pos_ref[1:2, :] + p_me * cb).astype(jnp.bfloat16)
+    valid = (dot(res_rows, row_pick) * dot(res_rows, col_pick))[0:1, :]
+
+    @pl.loop(1, nr)
+    def _(k):
+        q_copy(r_me, lax.rem(r_me + k, nr)).wait_recv()
+
+    @pl.loop(1, nd)
+    def _(k):
+        t = lax.rem(me + k, nd)
+        b_copy(r_me, p_me, t // nc, lax.rem(t, nc)).wait_recv()
+
+    first = (lax.broadcasted_iota(jnp.int32, (8, gw), 1) == 0).astype(f32)
+    mask_row = dot(first.astype(jnp.bfloat16), qrecv[:, 3 * gw :].astype(jnp.bfloat16), NT)[0:1]
+    key_bias = 1000000000.0 * (mask_row - 1.0)
+    for h in range(hpg):
+        queries = qrecv[:, h * depth : (h + 1) * depth] * depth ** (-0.5)
+        keys = qrecv[:, gw + h * depth : gw + (h + 1) * depth]
+        vals = qrecv[:, 2 * gw + h * depth : 2 * gw + (h + 1) * depth]
+        bias = jnp.concatenate([brecv[p, h] for p in range(nc)], axis=1)
+        scores = mm_high(queries, keys, NT) + bias + key_bias
+        weights = jnp.exp(scores - jnp.max(scores, axis=1, keepdims=True))
+        total = jnp.sum(weights, axis=1, keepdims=True)
+        msend[:, h * depth : (h + 1) * depth] = mm(weights, vals) / total
+
+    def m_copy(r, origin_r):
+        return copy(
+            2, msend.at[pl.ds(al(r * rb, rb), rb), :], mrecv.at[origin_r], r, origin_r, r, p_me
+        )
+
+    @pl.loop(1, nr)
+    def _(k):
+        m_copy(lax.rem(r_me + k, nr), r_me).start()
+
+    mrecv[r_me] = msend[pl.ds(al(r_me * rb, rb), rb), :]
+
+    @pl.loop(1, nr)
+    def _(k):
+        m_copy(r_me, lax.rem(r_me + k, nr)).wait_recv()
+
+    mixed = jnp.concatenate(
+        [
+            jnp.concatenate([mrecv[s * groups + g] for g in range(groups)], axis=1)
+            for s in range(sb)
+        ],
+        axis=0,
+    )
+    new_ali = ali + mm(mixed * gate, aout_ref[...])
+    factors = mm(layer_norm(new_ali), oin_ref[...])
+    width = sb * ow
+    lane = lax.broadcasted_iota(jnp.int32, (rb, 128), 1)
+    mask_lanes = jnp.zeros((rb, 128), f32)
+    for s in range(sb):
+        part = factors[s * rb : (s + 1) * rb] * mask_cols[s]
+        fls[:, s * ow : (s + 1) * ow] = part[:, :ow]
+        frs[:, s * ow : (s + 1) * ow] = part[:, ow:]
+        mask_lanes = jnp.where(lane == s, mask_cols[s], mask_lanes)
+    fls[:, width:] = mask_lanes
+    frs[:, width:] = mask_lanes
+    home = r_me // per
+
+    def fr_copy(r, p, origin_r, origin_p):
+        return copy(
+            3, frs, frr.at[origin_p, pl.ds(al(lax.rem(origin_r, per) * rb, rb), rb), :],
+            r, origin_r * nc + origin_p, r, p,
+        )
+
+    def fl_copy(p, origin_p):
+        return copy(4, fls, flr.at[origin_p], p, origin_p, r_me, p)
+
+    @pl.loop(0, nr)
+    def _(k):
+        r = lax.rem(r_me + k, nr)
+
+        @pl.when(jnp.logical_or(r != r_me, home != p_me))
+        def _():
+            fr_copy(r, home, r_me, p_me).start()
+
+    for k in range(1, nc):
+        fl_copy(lax.rem(p_me + k, nc), p_me).start()
+
+    nali_ref[...] = new_ali.reshape(sb, rb, cm)
+
+    @pl.when(home == p_me)
+    def _():
+        frr[p_me, pl.ds(al(lax.rem(r_me, per) * rb, rb), rb), :] = frs[...]
+
+    flr[p_me] = fls[...]
+
+    for k in range(1, nc):
+        fl_copy(p_me, lax.rem(p_me + k, nc)).wait_recv()
+
+    for p in range(nc):
+        for s in range(sb):
+            lsc[pl.ds(p * sb + s, rb, stride=seq), :] = jnp.concatenate(
+                [flr[p, :, s * ow : (s + 1) * ow], jnp.zeros((rb, 128 - ow), f32)], axis=1
+            )
+    left = lsc[:, :ow]
+    left_high, left_low = split(left)
+    left_cat = jnp.concatenate([left_high, left_low, left_high], axis=1)
+    for q in range(ow):
+        w_high, w_low = split(oout_ref[pl.ds(q, ow, stride=ow), :])
+        w_cat = jnp.concatenate([w_high, w_high, w_low], axis=0)
+        tsc[:, q, :, :] = dot(left_cat, w_cat).reshape(rb, seq, cz)
+
+    @pl.loop(0, per * nc)
+    def _(k):
+        origin_r = p_me * per + k // nc
+        origin_p = lax.rem(k, nc)
+
+        @pl.when(jnp.logical_or(origin_r != r_me, origin_p != p_me))
+        def _():
+            fr_copy(r_me, p_me, origin_r, origin_p).wait_recv()
+
+    right = pick_right(
+        split(jnp.concatenate([frr[p, :, :width] for p in range(nc)], axis=1)), perm_outer_ref[...]
+    )
+    mask_right = jnp.concatenate([frr[p, :, width : width + sb] for p in range(nc)], axis=1)
+    mask_left = jnp.concatenate([flr[p, :, width : width + sb] for p in range(nc)], axis=1)
+    for i in range(rb):
+        outer = dot_split(right, split(tsc[i].reshape(ow * seq, cz)))
+        count = jnp.sum(mask_right * mask_left[i : i + 1, :], axis=1, keepdims=True)
+        p1[i * cb : (i + 1) * cb, :] = pair_ref[i] + outer / (1.0 + count)
+    pair_one = p1[...]
+    tri_norm = layer_norm(pair_one)
+    tri_split = split(tri_norm)
+    edge = sigmoid(dot_split(w_gate, tri_split, NT)) * dot_split(w_value, tri_split, NT) * valid
+    for b in range(nib):
+        es[b] = edge[:, b * 128 : (b + 1) * 128]
+
+    rows_each = 2 * cpd
+
+    def e_copy(r, p, origin_r, origin_p):
+        return copy(
+            5, es.at[:, pl.ds(al((r * nc + p) * rows_each, rows_each), rows_each), :],
+            er.at[:, pl.ds(al((origin_p * nr + origin_r) * rows_each, rows_each), rows_each), :],
+            r * nc + p, origin_r * nc + origin_p, r, p,
+        )
+
+    @pl.loop(1, nd)
+    def _(k):
+        t = lax.rem(me + k, nd)
+        e_copy(t // nc, lax.rem(t, nc), r_me, p_me).start()
+
+    er[:, pl.ds(al((p_me * nr + r_me) * rows_each, rows_each), rows_each), :] = es[
+        :, pl.ds(al(me * rows_each, rows_each), rows_each), :
+    ]
+    out_gate = sigmoid(dot_split(tri_split, split(tgate_ref[...])))
+
+    @pl.loop(1, nd)
+    def _(k):
+        t = lax.rem(me + k, nd)
+        e_copy(r_me, p_me, t // nc, lax.rem(t, nc)).wait_recv()
+
+    def edge_matrix(row):
+        blocks = []
+        per_lane = 128 // cb
+        for b in range(nib):
+            halves = [er[b, pl.ds(p * nr * rows_each + row, nr, stride=rows_each), :] for p in range(nc)]
+            for n in range(per_lane):
+                blocks.append(
+                    jnp.concatenate([half[:, n * cb : (n + 1) * cb] for half in halves], axis=1)
+                )
+        return pick(perm_row_ref[...], split(jnp.concatenate(blocks, axis=0)))
+
+    for c in range(cpd):
+        crossed = dot_split(edge_matrix(c), edge_matrix(cpd + c), NT)
+        for p in range(nc):
+            cs[p, c] = crossed[:, p * cb : (p + 1) * cb]
+
+    def c_copy(r, p, origin):
+        return copy(
+            6, cs.at[p, :, pl.ds(al(r * rb, rb), rb), :], cr.at[pl.ds(origin * cpd, cpd)],
+            r * nc + p, origin, r, p,
+        )
+
+    @pl.loop(1, nd)
+    def _(k):
+        t = lax.rem(me + k, nd)
+        c_copy(t // nc, lax.rem(t, nc), me).start()
+
+    cr[pl.ds(me * cpd, cpd)] = cs[p_me, :, pl.ds(al(r_me * rb, rb), rb), :]
+
+    @pl.loop(1, nd)
+    def _(k):
+        t = lax.rem(me + k, nd)
+        c_copy(r_me, p_me, t).wait_recv()
+
+    crossed = cr[...]
+    center = crossed - jnp.mean(crossed, axis=0, keepdims=True)
+    spread = jnp.mean(center * center, axis=0, keepdims=True)
+    normed = (center * lax.rsqrt(spread + epsilon)).reshape(tri * rb, cb)
+    xs[...] = jnp.concatenate([normed] * (128 // cb), axis=1)
+    w_out = split(tout_ref[...])
+    tri_rows = []
+    for i in range(rb):
+        flipped = xs[pl.ds(i, tri, stride=rb), :].T[:cb]
+        tri_rows.append(dot_split(split(flipped), w_out))
+    triangle = jnp.concatenate(tri_rows, axis=0) * out_gate
+    pair_mid = pair_one + triangle
+    hidden = jnp.maximum(mm(layer_norm(pair_mid), xin_ref[...]), 0.0)
+    npair_ref[...] = (pair_mid + mm(hidden, xout_ref[...])).reshape(rb, cb, cz)
+
+    @pl.loop(1, nr)
+    def _(k):
+        r = lax.rem(r_me + k, nr)
+        q_copy(r, r_me).wait_send()
+        m_copy(r, r_me).wait_send()
+
+    @pl.loop(0, nr)
+    def _(k):
+        r = lax.rem(r_me + k, nr)
+
+        @pl.when(jnp.logical_or(r != r_me, home != p_me))
+        def _():
+            fr_copy(r, home, r_me, p_me).wait_send()
+
+    for k in range(1, nc):
+        fl_copy(lax.rem(p_me + k, nc), p_me).wait_send()
+
+    @pl.loop(1, nd)
+    def _(k):
+        t = lax.rem(me + k, nd)
+        b_copy(t // nc, lax.rem(t, nc), r_me, p_me).wait_send()
+        e_copy(t // nc, lax.rem(t, nc), r_me, p_me).wait_send()
+        c_copy(t // nc, lax.rem(t, nc), me).wait_send()
+
+
+def fused(sizes, *args):
+    (pair, ali, res_mask, row_mask, ain, pbw, aout, oin, oout, tin, tgate, tout, xin, xout) = args
+    nb, np_, nc = sizes
+    nr = nb * np_
+    nd = nr * nc
+    rb, cb, cz = pair.shape
+    sb, _, cm = ali.shape
+    res = rb * nr
+    seq = sb * nc
+    heads = pbw.shape[1]
+    depth = aout.shape[0] // heads
+    groups = nr // sb
+    hpg = heads // groups
+    gw = hpg * depth
+    ow = oin.shape[1] // 2
+    tri = tout.shape[0]
+    cpd = tri // nd
+    pos = rb * cb
+    f32 = jnp.float32
+
+    a = np.arange(seq * ow)
+    perm_outer = np.zeros((seq * ow, seq * ow), np.float32)
+    perm_outer[a, (a % ow) * seq + a // ow] = 1.0
+    row = np.arange(2 * tri)
+    channel = (row // cpd % 2) * 2 * tri + (row // (2 * cpd)) * cpd + row % cpd
+    perm_gate = np.zeros((2 * tri, 4 * tri), np.float32)
+    perm_gate[row, channel] = 1.0
+    perm_value = np.zeros((2 * tri, 4 * tri), np.float32)
+    perm_value[row, channel + tri] = 1.0
+    n = np.arange(res)
+    perm_row = np.zeros((res, res), np.float32)
+    perm_row[n, (n % rb) * nr + n // rb] = 1.0
+    position = np.arange(pos)
+    pos_table = np.stack([position // cb, position % cb]).astype(np.int32)
+    consts = [jnp.asarray(m, jnp.bfloat16) for m in (perm_outer, perm_gate, perm_value, perm_row)]
+    operands = [
+        pair, ali, res_mask.reshape(1, res), row_mask, ain, pbw, aout, oin, oout, tin, tgate, tout,
+        xin, xout, *consts, jnp.asarray(pos_table),
+    ]
+    vmem = pl.BlockSpec(memory_space=pltpu.VMEM)
+    fw = sb * ow + 128
+    scratch = [
+        ((nr, rb, 4 * gw)), ((res, 4 * gw)),
+        ((heads, rb, cb)), ((nc, hpg, res, cb)),
+        ((res, gw)), ((nr, rb, gw)),
+        ((rb, fw)), ((nc, cb, fw)), ((rb, fw)), ((nc, rb, fw)),
+        ((pos // 128, 2 * tri, 128)), ((pos // 128, 2 * tri, 128)),
+        ((nc, cpd, res, cb)), ((tri, rb, cb)),
+        ((rb * seq, 128)), ((rb, ow, seq, cz)), ((pos, cz)), ((tri * rb, 128)),
+    ]
+    return pl.pallas_call(
+        functools.partial(block_kernel, sizes),
+        out_shape=(
+            jax.ShapeDtypeStruct(ali.shape, f32),
+            jax.ShapeDtypeStruct(pair.shape, f32),
+        ),
+        in_specs=[vmem] * len(operands),
+        out_specs=(vmem, vmem),
+        scratch_shapes=[pltpu.VMEM(s, f32) for s in scratch]
+        + [pltpu.SemaphoreType.DMA((7, nd)), pltpu.SemaphoreType.DMA((7, nd))],
+        compiler_params=pltpu.CompilerParams(
+            collective_id=0, has_side_effects=True, vmem_limit_bytes=48 * 1024 * 1024
+        ),
+    )(*operands)
+
+
+def fits(sizes, args):
+    pair, ali, pbw, aout, oin, tout = (args[n] for n in (0, 1, 5, 6, 7, 11))
+    nb, np_, nc = sizes
+    nr = nb * np_
+    rb, cb, cz = pair.shape
+    sb = ali.shape[0]
+    heads = pbw.shape[1]
+    depth = aout.shape[0] // heads
+    if nr % sb or heads % (nr // sb) or nr % nc or tout.shape[0] % (nr * nc):
+        return False
+    return (
+        ali.shape[1] == rb and rb % 8 == 0 and cb * nc == rb * nr and 128 % cb == 0 and cz == 128
+        and (sb * nc) % 8 == 0 and (2 * (tout.shape[0] // (nr * nc))) % 8 == 0
+        and (heads // (nr // sb)) * depth * 4 % 128 == 0 and sb * (oin.shape[1] // 2) % 128 == 0
+        and (rb * cb) % 128 == 0
+    )
+
+
 def solution(mesh):
+    sizes = tuple(mesh.shape[name] for name in ("branch", "prow", "pcol"))
+
+    def local(*args):
+        if fits(sizes, args):
+            return fused(sizes, *args)
+        return shards(*args)
+
     return jax.shard_map(
-        shards,
+        local,
         mesh=mesh,
         in_specs=(
             P(("branch", "prow"), "pcol", None),

time: 267 us -> 79.7 us (0.30)
  blocking collectives: 113 us -> 0 us
  Pallas kernels: 0 us -> 62.4 us
  waiting for transfers between devices: 60.9 us -> 0 us
  matrix products: 39.3 us -> 0 us
  between operations: 14.2 us -> 0.71 us
  other arithmetic: 13.1 us -> 0 us
  starting transfers between devices: 6.64 us -> 0 us
  local copies, waits for them, and re-layouts: 18.5 us -> 15.8 us
    all_gather x6 -> x0, blocking collectives: 113 us -> none  [the longest x1 34.3 us: shards(): lax.all_gather(mask_float, ('branch', 'prow'), axis=1, tiled=True)]
    pallas_call x0 -> x1, Pallas kernels: none -> 62.4 us  [fused(): pl.pallas_call(functools.partial(block_kernel, sizes), out_shape=(jax.Sha...]
    all_gather x2 -> x0, waiting for transfers between devices: 48.1 us -> none  [the longest x1 48.1 us: shards(): lax.all_gather(right_edge, ('branch', 'prow'), axis=0, tiled=True)]
    dot_general x17 -> x0, matrix products: 39.3 us -> none  [the longest x11 16.8 us: matmul(): jnp.dot(left_side, right_side, precision=highest, preferred_element_type=...]
    unnamed x28 -> x38, local copies, waits for them, and re-layouts: 2.01 us -> 15.8 us
    reduce_scatter x1 -> x0, waiting for transfers between devices: 12.7 us -> none  [shards(): lax.psum_scatter(cross_part, 'pcol', scatter_dimension=1, tiled=True)]
    all_gather x5 -> x0, local copies, waits for them, and re-layouts: 9.48 us -> none  [the longest x1 9.12 us: shards(): lax.all_gather(right_edge, ('branch', 'prow'), axis=0, tiled=True)]
    reduce_sum x10 -> x0, other arithmetic: 7.28 us -> none  [the longest x6 4 us: layer_norm(): spread = jnp.mean(center * center, axis=-1, keepdims=True)]
  transfers between devices with their start and end apart: 5 -> 0, of which waited for: 2 -> 0; matrix products, arithmetic and copies ran while one was open for 4% -> 0% of each run, Pallas kernels for 0% -> 0%
where the time goes in v1:
time: 79.7 us; the launch traced here: 79 us
  Pallas kernels  62.4 us (78%)
  local copies, waits for them, and re-layouts  15.8 us (20%)
    pallas_call x1, Pallas kernels, fused(): pl.pallas_call(functools.partial(block_kernel, sizes), out_shape=(jax.Sha...  62.4 us
    unnamed x38, local copies, waits for them, and re-layouts  15.8 us

profile of v1, /device:TPU:0, one launch (start us, length us, event | category | flops | bytes accessed | tf_op | source)
XLA Modules:
  0.0 79.0 jit_solution(11982621788127245438)
XLA Ops:
  0.6 0.0 copy-start.2
  0.6 0.8 %copy.21.pbw_ref = f32[128,8]{1,0:T(8,128)S(1)} copy(f32[128,8]{0,1:T(8,128)} %param.24) | data formatting | bytes 8192 | tf_op args[5]
  1.5 0.0 copy-start.14
  1.5 0.0 copy-start.16
  1.5 0.9 %copy.22.oin_ref = f32[256,64]{1,0:T(8,128)S(1)} copy(f32[256,64]{0,1:T(8,128)} %param.26) | data formatting | bytes 131072 | tf_op args[7]
  2.4 0.0 copy-done.2
  2.4 0.0 copy-done.14
  2.5 0.0 copy-done.16
  2.5 0.0 copy-start
  2.5 1.2 %copy-done = f32[256,1024]{1,0:T(8,128)S(1)} copy-done((f32[256,1024]{1,0:T(8,128)S(1)}, f32[256,1024]{1,0:T(8,128)}, u32[]{:S(2)}) %copy-start) | copy-done | bytes 1048600
  3.7 0.0 copy-start.1
  3.7 1.0 %copy-done.1 = f32[1024,128]{1,0:T(8,128)S(1)} copy-done((f32[1024,128]{1,0:T(8,128)S(1)}, f32[1024,128]{1,0:T(8,128)}, u32[]{:S(2)}) %copy-start.1) | copy-done | bytes 524312
  4.7 0.0 copy-start.3
  4.7 0.9 %copy-done.3 = f32[256,256]{1,0:T(8,128)S(1)} copy-done((f32[256,256]{1,0:T(8,128)S(1)}, f32[256,256]{1,0:T(8,128)}, u32[]{:S(2)}) %copy-start.3) | copy-done | bytes 262168
  5.7 0.0 copy-start.4
  5.7 0.9 %copy-done.4 = f32[128,512]{1,0:T(8,128)S(1)} copy-done((f32[128,512]{1,0:T(8,128)S(1)}, f32[128,512]{1,0:T(8,128)}, u32[]{:S(2)}) %copy-start.4) | copy-done | bytes 262168
  6.6 0.0 copy-start.5
  6.6 0.9 %copy-done.5 = f32[128,512]{1,0:T(8,128)S(1)} copy-done((f32[128,512]{1,0:T(8,128)S(1)}, f32[128,512]{1,0:T(8,128)}, u32[]{:S(2)}) %copy-start.5) | copy-done | bytes 262168
  7.6 0.0 copy-start.6
  7.6 0.9 %copy-done.6 = f32[512,128]{1,0:T(8,128)S(1)} copy-done((f32[512,128]{1,0:T(8,128)S(1)}, f32[512,128]{1,0:T(8,128)}, u32[]{:S(2)}) %copy-start.6) | copy-done | bytes 262168
  8.5 0.9 %copy-done.7 = bf16[256,512]{1,0:T(8,128)(2,1)S(1)} copy-done((bf16[256,512]{1,0:T(8,128)(2,1)S(1)}, bf16[256,512]{1,0:T(8,128)(2,1)}, u32[]{:S(2)}) %copy-start.7) | copy-done | bytes 262168
  9.5 0.0 copy-start.8
  9.5 0.9 %copy-done.8 = bf16[256,512]{1,0:T(8,128)(2,1)S(1)} copy-done((bf16[256,512]{1,0:T(8,128)(2,1)S(1)}, bf16[256,512]{1,0:T(8,128)(2,1)}, u32[]{:S(2)}) %copy-start.8) | copy-done | bytes 262168
  10.4 0.9 %copy-done.9 = bf16[256,256]{1,0:T(8,128)(2,1)S(1)} copy-done((bf16[256,256]{1,0:T(8,128)(2,1)S(1)}, bf16[256,256]{1,0:T(8,128)(2,1)}, u32[]{:S(2)}) %copy-start.9) | copy-done | bytes 131096
  11.3 0.8 %copy-done.10 = f32[128,128]{1,0:T(8,128)S(1)} copy-done((f32[128,128]{1,0:T(8,128)S(1)}, f32[128,128]{1,0:T(8,128)}, u32[]{:S(2)}) %copy-start.10) | copy-done | bytes 65560
  12.2 0.8 %copy-done.11 = f32[128,128]{1,0:T(8,128)S(1)} copy-done((f32[128,128]{1,0:T(8,128)S(1)}, f32[128,128]{1,0:T(8,128)}, u32[]{:S(2)}) %copy-start.11) | copy-done | bytes 65560
  13.0 0.8 copy-done.12
  13.8 0.8 copy-done.13
  14.5 0.7 copy-done.15
  15.2 62.4 %shard_map.194 = (f32[4,8,256]{2,1,0:T(8,128)S(1)}, f32[8,64,128]{2,1,0:T(8,128)S(1)}) custom-call(f32[8,64,128]{2,1,0:T(8,128)S(1)} %copy-done.2, f32[4,8,256]{2,1,0:T(8,128)S(1)} %copy-done.12, s32[1,128]{1,0:T(1,128)S(1)} %bitcast.1, s32[4,8]{1,0:T(4,128)S(1)} %copy-done.15, f32[256,1024]{1,0:T(8,128)S(1)} %copy-done, f32[128,8]{1,0:T(8,128)S(1)} %copy.21.pbw_ref, ...), custom_call_target="tpu_custom_call" | custom-call | tf_op jit(solution)/shard_map/pallas_call | solution.py:561
  77.7 0.6 copy.25
  78.3 0.7 copy.26
  (7 shorter events, 0.0 us)
Async XLA Ops:
  0.6 1.8 %copy-start.2 = (f32[8,64,128]{2,1,0:T(8,128)S(1)}, f32[8,64,128]{2,1,0:T(8,128)}, u32[]{:S(2)}) copy-start(f32[8,64,128]{2,1,0:T(8,128)} %pair_ref.1) | copy-start | bytes 786436
  1.5 1.0 %copy-start.14 = (s32[2,512]{1,0:T(2,128)S(1)}, s32[2,512]{1,0:T(2,128)}, u32[]{:S(2)}) copy-start(s32[2,512]{1,0:T(2,128)} %constant.14.clone.pos_ref) | copy-start | bytes 12292
  1.5 1.0 %copy-start.16 = (s32[128]{0:T(128)S(1)}, s32[128]{0:T(128)}, u32[]{:S(2)}) copy-start(s32[128]{0:T(128)} %param.21) | copy-start | bytes 1540
  2.5 1.2 %copy-start = (f32[256,1024]{1,0:T(8,128)S(1)}, f32[256,1024]{1,0:T(8,128)}, u32[]{:S(2)}) copy-start(f32[256,1024]{1,0:T(8,128)} %ain_ref.1) | copy-start | bytes 3145732
  3.7 1.0 %copy-start.1 = (f32[1024,128]{1,0:T(8,128)S(1)}, f32[1024,128]{1,0:T(8,128)}, u32[]{:S(2)}) copy-start(f32[1024,128]{1,0:T(8,128)} %oout_ref.1) | copy-start | bytes 1572868
  4.7 0.9 %copy-start.3 = (f32[256,256]{1,0:T(8,128)S(1)}, f32[256,256]{1,0:T(8,128)}, u32[]{:S(2)}) copy-start(f32[256,256]{1,0:T(8,128)} %aout_ref.1) | copy-start | bytes 786436
  5.7 0.9 %copy-start.4 = (f32[128,512]{1,0:T(8,128)S(1)}, f32[128,512]{1,0:T(8,128)}, u32[]{:S(2)}) copy-start(f32[128,512]{1,0:T(8,128)} %tin_ref.1) | copy-start | bytes 786436
  6.6 0.9 %copy-start.5 = (f32[128,512]{1,0:T(8,128)S(1)}, f32[128,512]{1,0:T(8,128)}, u32[]{:S(2)}) copy-start(f32[128,512]{1,0:T(8,128)} %xin_ref.1) | copy-start | bytes 786436
  7.6 0.9 %copy-start.6 = (f32[512,128]{1,0:T(8,128)S(1)}, f32[512,128]{1,0:T(8,128)}, u32[]{:S(2)}) copy-start(f32[512,128]{1,0:T(8,128)} %xout_ref.1) | copy-start | bytes 786436
  8.5 0.9 %copy-start.7 = (bf16[256,512]{1,0:T(8,128)(2,1)S(1)}, bf16[256,512]{1,0:T(8,128)(2,1)}, u32[]{:S(2)}) copy-start(bf16[256,512]{1,0:T(8,128)(2,1)} %constant.12.clone.perm_value_ref) | copy-start | bytes 786436
  9.5 0.9 %copy-start.8 = (bf16[256,512]{1,0:T(8,128)(2,1)S(1)}, bf16[256,512]{1,0:T(8,128)(2,1)}, u32[]{:S(2)}) copy-start(bf16[256,512]{1,0:T(8,128)(2,1)} %constant.11.clone.perm_gate_ref) | copy-start | bytes 786436
  10.4 0.9 %copy-start.9 = (bf16[256,256]{1,0:T(8,128)(2,1)S(1)}, bf16[256,256]{1,0:T(8,128)(2,1)}, u32[]{:S(2)}) copy-start(bf16[256,256]{1,0:T(8,128)(2,1)} %constant.10.clone.perm_outer_ref) | copy-start | bytes 393220
  11.3 0.8 %copy-start.10 = (f32[128,128]{1,0:T(8,128)S(1)}, f32[128,128]{1,0:T(8,128)}, u32[]{:S(2)}) copy-start(f32[128,128]{1,0:T(8,128)} %tgate_ref.1) | copy-start | bytes 196612
  12.2 0.8 %copy-start.11 = (f32[128,128]{1,0:T(8,128)S(1)}, f32[128,128]{1,0:T(8,128)}, u32[]{:S(2)}) copy-start(f32[128,128]{1,0:T(8,128)} %tout_ref.1) | copy-start | bytes 196612
  13.0 0.8 copy-start.12
  13.8 0.8 copy-start.13
  14.5 0.7 copy-start.15

commit v2 on v1

--- a/solution.py
+++ b/solution.py
@@ -171,15 +171,24 @@
     return tuple(dot(part, matrix).astype(jnp.bfloat16) for part in pair)
 
 
-def block_kernel(
-    sizes,
-    pair_ref, ali_ref, res_ref, row_ref, ain_ref, pbw_ref, aout_ref, oin_ref, oout_ref,
-    tin_ref, tgate_ref, tout_ref, xin_ref, xout_ref,
-    perm_outer_ref, perm_gate_ref, perm_value_ref, perm_row_ref, pos_ref,
-    nali_ref, npair_ref,
-    qsend, qrecv, bsend, brecv, msend, mrecv, frs, frr, fls, flr, es, er, cs, cr,
-    lsc, tsc, p1, xs, send_sem, recv_sem,
-):
+LOAD_ORDER = (0, 5, 1, 4, 3, 9, 15, 16, 2, 18, 6, 7, 8, 14, 10, 17, 11, 12, 13)
+
+
+def block_kernel(sizes, count, *refs):
+    hbm, outs, local = refs[:count], refs[count : count + 2], refs[count + 2 : 2 * count + 2]
+    (
+        pair_ref, ali_ref, res_ref, row_ref, ain_ref, pbw_ref, aout_ref, oin_ref, oout_ref,
+        tin_ref, tgate_ref, tout_ref, xin_ref, xout_ref,
+        perm_outer_ref, perm_gate_ref, perm_value_ref, perm_row_ref, pos_ref,
+    ) = local
+    nali_ref, npair_ref = outs
+    (
+        qsend, qrecv, bsend, brecv, msend, mrecv, frs, frr, fls, flr, es, er, cs, cr,
+        lsc, tsc, p1, send_sem, recv_sem, load_sem,
+    ) = refs[2 * count + 2 :]
+    loads = [pltpu.make_async_copy(a, b, load_sem.at[n]) for n, (a, b) in enumerate(zip(hbm, local))]
+    for n in LOAD_ORDER:
+        loads[n].start()
     nb, np_, nc = sizes
     nr = nb * np_
     nd = nr * nc
@@ -187,18 +196,22 @@
     sb, _, cm = ali_ref.shape
     seq = sb * nc
     res = rb * nr
-    heads = pbw_ref.shape[1]
+    heads = pbw_ref.shape[0]
     att = aout_ref.shape[0]
     depth = att // heads
     groups = nr // sb
     hpg = heads // groups
     gw = hpg * depth
-    ow = oin_ref.shape[1] // 2
+    ow = oin_ref.shape[0] // 2
     tri = tout_ref.shape[0]
     cpd = tri // nd
     per = nr // nc
     pos = rb * cb
     nib = pos // 128
+    per_lane = 128 // cb
+    order = [b * per_lane + n for n in range(per_lane) for b in range(nib)]
+    brows = hpg * nib
+    crows = cpd * nib
     f32 = jnp.float32
 
     r_me = lax.axis_index("branch") * np_ + lax.axis_index("prow")
@@ -224,18 +237,21 @@
         t = lax.rem(me + k, nd)
         pl.semaphore_signal(barrier, inc=1, device_id=where(t // nc, lax.rem(t, nc)), device_id_type=MESH)
 
+    loads[0].wait()
+    loads[5].wait()
     pair = pair_ref[...].reshape(pos, cz)
     pair_norm = layer_norm(pair)
-    for i in range(rb):
-        bsend[:, i, :] = mm_high(pbw_ref[...].T, pair_norm[i * cb : (i + 1) * cb], NT)
+    bias_rows = mm_high(pbw_ref[...], pair_norm, NT)
+    for b in range(nib):
+        bsend[pl.ds(b, heads, stride=nib), :] = bias_rows[:, b * 128 : (b + 1) * 128]
 
     pl.semaphore_wait(barrier, nd - 1)
 
     def b_copy(r, p, origin_r, origin_p):
         group = lax.rem(r, groups)
         return copy(
-            1, bsend.at[pl.ds(group * hpg, hpg)],
-            brecv.at[origin_p, :, pl.ds(al(origin_r * rb, rb), rb), :],
+            1, bsend.at[pl.ds(al(group * brows, brows), brows), :],
+            brecv.at[origin_p, pl.ds(al(origin_r * brows, brows), brows), :],
             r * nc + p, origin_r * nc + origin_p, r, p,
         )
 
@@ -244,10 +260,15 @@
         t = lax.rem(me + k, nd)
         b_copy(t // nc, lax.rem(t, nc), r_me, p_me).start()
 
-    brecv[p_me, :, pl.ds(al(r_me * rb, rb), rb), :] = bsend[pl.ds(lax.rem(r_me, groups) * hpg, hpg)]
-
+    brecv[p_me, pl.ds(al(r_me * brows, brows), brows), :] = bsend[
+        pl.ds(al(lax.rem(r_me, groups) * brows, brows), brows), :
+    ]
+
+    loads[1].wait()
+    loads[4].wait()
+    loads[3].wait()
     ali = ali_ref[...].reshape(sb * rb, cm)
-    projected = mm_high(layer_norm(ali), ain_ref[...])
+    projected = mm(layer_norm(ali), ain_ref[...])
     gate = sigmoid(projected[:, 3 * att :])
     mask = row_ref[...].astype(f32)
     eye = (
@@ -274,6 +295,11 @@
 
     qrecv[pl.ds(al(r_me * rb, rb), rb), :] = qsend[r_me]
 
+    loads[9].wait()
+    loads[15].wait()
+    loads[16].wait()
+    loads[2].wait()
+    loads[18].wait()
     tin = split(tin_ref[...])
     w_gate = pick(perm_gate_ref[...], tin, NT)
     w_value = pick(perm_value_ref[...], tin, NT)
@@ -295,15 +321,32 @@
     first = (lax.broadcasted_iota(jnp.int32, (8, gw), 1) == 0).astype(f32)
     mask_row = dot(first.astype(jnp.bfloat16), qrecv[:, 3 * gw :].astype(jnp.bfloat16), NT)[0:1]
     key_bias = 1000000000.0 * (mask_row - 1.0)
+    msend[...] = qrecv[:, 0:128]
+    query_rows = jnp.concatenate([msend[pl.ds(i, nr, stride=rb), :] for i in order], axis=0)
+    mixed_heads = []
     for h in range(hpg):
-        queries = qrecv[:, h * depth : (h + 1) * depth] * depth ** (-0.5)
+        queries = query_rows[:, h * depth : (h + 1) * depth] * depth ** (-0.5)
         keys = qrecv[:, gw + h * depth : gw + (h + 1) * depth]
         vals = qrecv[:, 2 * gw + h * depth : 2 * gw + (h + 1) * depth]
-        bias = jnp.concatenate([brecv[p, h] for p in range(nc)], axis=1)
+        tiles = [
+            [brecv[p, pl.ds(h * nib + b, nr, stride=brows), :] for p in range(nc)] for b in range(nib)
+        ]
+        bias = jnp.concatenate(
+            [
+                jnp.concatenate([half[:, n * cb : (n + 1) * cb] for half in tiles[b]], axis=1)
+                for n in range(per_lane)
+                for b in range(nib)
+            ],
+            axis=0,
+        )
         scores = mm_high(queries, keys, NT) + bias + key_bias
         weights = jnp.exp(scores - jnp.max(scores, axis=1, keepdims=True))
         total = jnp.sum(weights, axis=1, keepdims=True)
-        msend[:, h * depth : (h + 1) * depth] = mm(weights, vals) / total
+        mixed_heads.append(mm(weights, vals) / total)
+    mixed_heads.append(jnp.zeros((res, 128 - gw), f32))
+    mixed_rows = jnp.concatenate(mixed_heads, axis=1)
+    for n, i in enumerate(order):
+        msend[pl.ds(i, nr, stride=rb), :] = mixed_rows[n * nr : (n + 1) * nr]
 
     def m_copy(r, origin_r):
         return copy(
@@ -322,13 +365,15 @@
 
     mixed = jnp.concatenate(
         [
-            jnp.concatenate([mrecv[s * groups + g] for g in range(groups)], axis=1)
+            jnp.concatenate([mrecv[s * groups + g, :, :gw] for g in range(groups)], axis=1)
             for s in range(sb)
         ],
         axis=0,
     )
+    loads[6].wait()
+    loads[7].wait()
     new_ali = ali + mm(mixed * gate, aout_ref[...])
-    factors = mm(layer_norm(new_ali), oin_ref[...])
+    factors = mm(layer_norm(new_ali), oin_ref[...], NT)
     width = sb * ow
     lane = lax.broadcasted_iota(jnp.int32, (rb, 128), 1)
     mask_lanes = jnp.zeros((rb, 128), f32)
@@ -380,6 +425,7 @@
     left = lsc[:, :ow]
     left_high, left_low = split(left)
     left_cat = jnp.concatenate([left_high, left_low, left_high], axis=1)
+    loads[8].wait()
     for q in range(ow):
         w_high, w_low = split(oout_ref[pl.ds(q, ow, stride=ow), :])
         w_cat = jnp.concatenate([w_high, w_high, w_low], axis=0)
@@ -394,6 +440,7 @@
         def _():
             fr_copy(r_me, p_me, origin_r, origin_p).wait_recv()
 
+    loads[14].wait()
     right = pick_right(
         split(jnp.concatenate([frr[p, :, :width] for p in range(nc)], axis=1)), perm_outer_ref[...]
     )
@@ -427,6 +474,11 @@
     er[:, pl.ds(al((p_me * nr + r_me) * rows_each, rows_each), rows_each), :] = es[
         :, pl.ds(al(me * rows_each, rows_each), rows_each), :
     ]
+    loads[10].wait()
+    loads[17].wait()
+    loads[11].wait()
+    loads[12].wait()
+    loads[13].wait()
     out_gate = sigmoid(dot_split(tri_split, split(tgate_ref[...])))
 
     @pl.loop(1, nd)
@@ -434,25 +486,33 @@
         t = lax.rem(me + k, nd)
         e_copy(r_me, p_me, t // nc, lax.rem(t, nc)).wait_recv()
 
-    def edge_matrix(row):
+    def edge_blocks(row):
         blocks = []
-        per_lane = 128 // cb
         for b in range(nib):
             halves = [er[b, pl.ds(p * nr * rows_each + row, nr, stride=rows_each), :] for p in range(nc)]
             for n in range(per_lane):
                 blocks.append(
                     jnp.concatenate([half[:, n * cb : (n + 1) * cb] for half in halves], axis=1)
                 )
-        return pick(perm_row_ref[...], split(jnp.concatenate(blocks, axis=0)))
+        return blocks
 
     for c in range(cpd):
-        crossed = dot_split(edge_matrix(c), edge_matrix(cpd + c), NT)
+        blocks = edge_blocks(c)
+        left_rows = split(jnp.concatenate([blocks[i] for i in order], axis=0))
+        right_rows = pick(perm_row_ref[...], split(jnp.concatenate(edge_blocks(cpd + c), axis=0)))
+        crossed = dot_split(left_rows, right_rows, NT)
         for p in range(nc):
-            cs[p, c] = crossed[:, p * cb : (p + 1) * cb]
+            half = crossed[:, p * cb : (p + 1) * cb]
+            packed = jnp.concatenate(
+                [half[n * nib * nr : (n + 1) * nib * nr] for n in range(per_lane)], axis=1
+            )
+            for b in range(nib):
+                cs[p, pl.ds(c * nib + b, nr, stride=crows), :] = packed[b * nr : (b + 1) * nr]
 
     def c_copy(r, p, origin):
         return copy(
-            6, cs.at[p, :, pl.ds(al(r * rb, rb), rb), :], cr.at[pl.ds(origin * cpd, cpd)],
+            6, cs.at[p, pl.ds(al(r * crows, crows), crows), :],
+            cr.at[pl.ds(al(origin * crows, crows), crows), :],
             r * nc + p, origin, r, p,
         )
 
@@ -461,23 +521,18 @@
         t = lax.rem(me + k, nd)
         c_copy(t // nc, lax.rem(t, nc), me).start()
 
-    cr[pl.ds(me * cpd, cpd)] = cs[p_me, :, pl.ds(al(r_me * rb, rb), rb), :]
+    cr[pl.ds(al(me * crows, crows), crows), :] = cs[p_me, pl.ds(al(r_me * crows, crows), crows), :]
 
     @pl.loop(1, nd)
     def _(k):
         t = lax.rem(me + k, nd)
         c_copy(r_me, p_me, t).wait_recv()
 
-    crossed = cr[...]
-    center = crossed - jnp.mean(crossed, axis=0, keepdims=True)
-    spread = jnp.mean(center * center, axis=0, keepdims=True)
-    normed = (center * lax.rsqrt(spread + epsilon)).reshape(tri * rb, cb)
-    xs[...] = jnp.concatenate([normed] * (128 // cb), axis=1)
     w_out = split(tout_ref[...])
     tri_rows = []
-    for i in range(rb):
-        flipped = xs[pl.ds(i, tri, stride=rb), :].T[:cb]
-        tri_rows.append(dot_split(split(flipped), w_out))
+    for b in range(nib):
+        channels = cr[pl.ds(b, tri, stride=nib), :]
+        tri_rows.append(dot_split(split(layer_norm(channels.T)), w_out))
     triangle = jnp.concatenate(tri_rows, axis=0) * out_gate
     pair_mid = pair_one + triangle
     hidden = jnp.maximum(mm(layer_norm(pair_mid), xin_ref[...]), 0.0)
@@ -526,6 +581,7 @@
     tri = tout.shape[0]
     cpd = tri // nd
     pos = rb * cb
+    nib = pos // 128
     f32 = jnp.float32
 
     a = np.arange(seq * ow)
@@ -544,32 +600,34 @@
     pos_table = np.stack([position // cb, position % cb]).astype(np.int32)
     consts = [jnp.asarray(m, jnp.bfloat16) for m in (perm_outer, perm_gate, perm_value, perm_row)]
     operands = [
-        pair, ali, res_mask.reshape(1, res), row_mask, ain, pbw, aout, oin, oout, tin, tgate, tout,
+        pair, ali, res_mask.reshape(1, res), row_mask, ain, pbw.T, aout, oin.T, oout, tin, tgate, tout,
         xin, xout, *consts, jnp.asarray(pos_table),
     ]
     vmem = pl.BlockSpec(memory_space=pltpu.VMEM)
     fw = sb * ow + 128
     scratch = [
         ((nr, rb, 4 * gw)), ((res, 4 * gw)),
-        ((heads, rb, cb)), ((nc, hpg, res, cb)),
-        ((res, gw)), ((nr, rb, gw)),
+        ((heads * nib, 128)), ((nc, nr * hpg * nib, 128)),
+        ((res, 128)), ((nr, rb, 128)),
         ((rb, fw)), ((nc, cb, fw)), ((rb, fw)), ((nc, rb, fw)),
         ((pos // 128, 2 * tri, 128)), ((pos // 128, 2 * tri, 128)),
-        ((nc, cpd, res, cb)), ((tri, rb, cb)),
-        ((rb * seq, 128)), ((rb, ow, seq, cz)), ((pos, cz)), ((tri * rb, 128)),
+        ((nc, nr * cpd * nib, 128)), ((tri * nib, 128)),
+        ((rb * seq, 128)), ((rb, ow, seq, cz)), ((pos, cz)),
     ]
     return pl.pallas_call(
-        functools.partial(block_kernel, sizes),
+        functools.partial(block_kernel, sizes, len(operands)),
         out_shape=(
             jax.ShapeDtypeStruct(ali.shape, f32),
             jax.ShapeDtypeStruct(pair.shape, f32),
         ),
-        in_specs=[vmem] * len(operands),
+        in_specs=[pl.BlockSpec(memory_space=pltpu.HBM)] * len(operands),
         out_specs=(vmem, vmem),
-        scratch_shapes=[pltpu.VMEM(s, f32) for s in scratch]
-        + [pltpu.SemaphoreType.DMA((7, nd)), pltpu.SemaphoreType.DMA((7, nd))],
+        scratch_shapes=[pltpu.VMEM(m.shape, m.dtype) for m in operands]
+        + [pltpu.VMEM(s, f32) for s in scratch]
+        + [pltpu.SemaphoreType.DMA((7, nd)), pltpu.SemaphoreType.DMA((7, nd))]
+        + [pltpu.SemaphoreType.DMA((len(operands),))],
         compiler_params=pltpu.CompilerParams(
-            collective_id=0, has_side_effects=True, vmem_limit_bytes=48 * 1024 * 1024
+            collective_id=0, has_side_effects=True, vmem_limit_bytes=63 * 1024 * 1024
         ),
     )(*operands)
 
@@ -588,7 +646,9 @@
         ali.shape[1] == rb and rb % 8 == 0 and cb * nc == rb * nr and 128 % cb == 0 and cz == 128
         and (sb * nc) % 8 == 0 and (2 * (tout.shape[0] // (nr * nc))) % 8 == 0
         and (heads // (nr // sb)) * depth * 4 % 128 == 0 and sb * (oin.shape[1] // 2) % 128 == 0
-        and (rb * cb) % 128 == 0
+        and rb % (128 // cb) == 0 and (heads // (nr // sb)) * depth * 2 == 128
+        and (heads // (nr // sb)) * (rb * cb // 128) % 8 == 0
+        and tout.shape[0] // (nr * nc) * (rb * cb // 128) % 8 == 0
     )
 
 

time: 79.7 us -> 60.1 us (0.75)
  local copies, waits for them, and re-layouts: 15.8 us -> 3.05 us
  Pallas kernels: 62.4 us -> 56.2 us
    unnamed x38 -> x2, local copies, waits for them, and re-layouts: 15.8 us -> 3.05 us
    pallas_call x1, Pallas kernels: 62.4 us -> 56.2 us  [fused(): pl.pallas_call(functools.partial(block_kernel, sizes, len(operands)), out...]
where the time goes in v2:
time: 60.1 us; the launch traced here: 59.9 us
  Pallas kernels  56.2 us (94%)
  local copies, waits for them, and re-layouts  3.05 us (5%)
  between operations  0.64 us (1%)
    pallas_call x1, Pallas kernels, fused(): pl.pallas_call(functools.partial(block_kernel, sizes, len(operands)), out...  56.2 us
    unnamed x2, local copies, waits for them, and re-layouts  3.05 us

profile of v2, /device:TPU:0, one launch (start us, length us, event | category | flops | bytes accessed | tf_op | source)
XLA Modules:
  0.0 59.9 jit_solution(5866951864956075095)
XLA Ops:
  0.6 56.2 %shard_map.194 = (f32[4,8,256]{2,1,0:T(8,128)}, f32[8,64,128]{2,1,0:T(8,128)}) custom-call(f32[8,64,128]{2,1,0:T(8,128)} %refs_0_.1, f32[4,8,256]{2,1,0:T(8,128)} %refs_1_.1, s32[1,128]{1,0:T(1,128)} %bitcast.5, s32[4,8]{1,0:T(4,128)} %refs_3_.1, f32[256,1024]{1,0:T(8,128)} %refs_4_.1, f32[8,128]{1,0:T(8,128)} %bitcast.4, f32[256,256]{1,0:T(8,128)} %refs_6_.1, ...), custom_call_target="tpu_custom_call" | custom-call | tf_op jit(solution)/shard_map/pallas_call | solution.py:617
  56.8 1.4 %copy.23 = f32[4,8,256]{2,1,0:T(8,128)} copy(f32[4,8,256]{2,1,0:T(8,128)} %get-tuple-element.4) | data formatting | bytes 65536
  58.2 1.7 %copy.24 = f32[8,64,128]{2,1,0:T(8,128)} copy(f32[8,64,128]{2,1,0:T(8,128)} %get-tuple-element.5) | data formatting | bytes 524288

commit v3 on v2

--- a/solution.py
+++ b/solution.py
@@ -148,6 +148,14 @@
 
 
 def dot_split(a, b, dims=NN):
+    rows, depth = a[0].shape
+    if rows <= 64:
+        both = dot(jnp.concatenate(a, axis=0), b[0], dims)
+        return both[:rows] + (both[rows:] + dot(a[0], b[1], dims))
+    if depth == 128:
+        axis = dims[0][1][0]
+        twice = dot(jnp.concatenate(a, axis=1), jnp.concatenate([b[0], b[0]], axis=axis), dims)
+        return twice + dot(a[0], b[1], dims)
     return dot(a[0], b[0], dims) + (dot(a[0], b[1], dims) + dot(a[1], b[0], dims))
 
 
@@ -171,6 +179,8 @@
     return tuple(dot(part, matrix).astype(jnp.bfloat16) for part in pair)
 
 
+EDGE_CHUNKS = 1
+CROSS_CHUNKS = 1
 LOAD_ORDER = (0, 5, 1, 4, 3, 9, 15, 16, 2, 18, 6, 7, 8, 14, 10, 17, 11, 12, 13)
 
 
@@ -184,7 +194,7 @@
     nali_ref, npair_ref = outs
     (
         qsend, qrecv, bsend, brecv, msend, mrecv, frs, frr, fls, flr, es, er, cs, cr,
-        lsc, tsc, p1, send_sem, recv_sem, load_sem,
+        lsc, tsc, p1, wcat, send_sem, recv_sem, load_sem,
     ) = refs[2 * count + 2 :]
     loads = [pltpu.make_async_copy(a, b, load_sem.at[n]) for n, (a, b) in enumerate(zip(hbm, local))]
     for n in LOAD_ORDER:
@@ -303,11 +313,21 @@
     tin = split(tin_ref[...])
     w_gate = pick(perm_gate_ref[...], tin, NT)
     w_value = pick(perm_value_ref[...], tin, NT)
+    w_edges = tuple(jnp.concatenate(half, axis=0) for half in zip(w_gate, w_value))
     res_rows = jnp.broadcast_to(res_ref[...].astype(f32), (8, res)).astype(jnp.bfloat16)
     index = lax.broadcasted_iota(jnp.int32, (res, pos), 0)
     row_pick = (index == pos_ref[0:1, :] + r_me * rb).astype(jnp.bfloat16)
     col_pick = (index == pos_ref[1:2, :] + p_me * cb).astype(jnp.bfloat16)
     valid = (dot(res_rows, row_pick) * dot(res_rows, col_pick))[0:1, :]
+
+    loads[6].wait()
+    loads[7].wait()
+    loads[8].wait()
+    w_att = split(aout_ref[...])
+    w_factor = split(oin_ref[...])
+    for q in range(ow):
+        w_high, w_low = split(oout_ref[pl.ds(q, ow, stride=ow), :])
+        wcat[q] = jnp.concatenate([w_high, w_high, w_low], axis=0)
 
     @pl.loop(1, nr)
     def _(k):
@@ -370,10 +390,8 @@
         ],
         axis=0,
     )
-    loads[6].wait()
-    loads[7].wait()
-    new_ali = ali + mm(mixed * gate, aout_ref[...])
-    factors = mm(layer_norm(new_ali), oin_ref[...], NT)
+    new_ali = ali + dot_split(split(mixed * gate), w_att)
+    factors = dot_split(split(layer_norm(new_ali)), w_factor, NT)
     width = sb * ow
     lane = lax.broadcasted_iota(jnp.int32, (rb, 128), 1)
     mask_lanes = jnp.zeros((rb, 128), f32)
@@ -425,11 +443,8 @@
     left = lsc[:, :ow]
     left_high, left_low = split(left)
     left_cat = jnp.concatenate([left_high, left_low, left_high], axis=1)
-    loads[8].wait()
     for q in range(ow):
-        w_high, w_low = split(oout_ref[pl.ds(q, ow, stride=ow), :])
-        w_cat = jnp.concatenate([w_high, w_high, w_low], axis=0)
-        tsc[:, q, :, :] = dot(left_cat, w_cat).reshape(rb, seq, cz)
+        tsc[:, q, :, :] = dot(left_cat, wcat[q]).reshape(rb, seq, cz)
 
     @pl.loop(0, per * nc)
     def _(k):
@@ -446,30 +461,39 @@
     )
     mask_right = jnp.concatenate([frr[p, :, width : width + sb] for p in range(nc)], axis=1)
     mask_left = jnp.concatenate([flr[p, :, width : width + sb] for p in range(nc)], axis=1)
-    for i in range(rb):
-        outer = dot_split(right, split(tsc[i].reshape(ow * seq, cz)))
-        count = jnp.sum(mask_right * mask_left[i : i + 1, :], axis=1, keepdims=True)
-        p1[i * cb : (i + 1) * cb, :] = pair_ref[i] + outer / (1.0 + count)
-    pair_one = p1[...]
-    tri_norm = layer_norm(pair_one)
-    tri_split = split(tri_norm)
-    edge = sigmoid(dot_split(w_gate, tri_split, NT)) * dot_split(w_value, tri_split, NT) * valid
-    for b in range(nib):
-        es[b] = edge[:, b * 128 : (b + 1) * 128]
-
     rows_each = 2 * cpd
-
-    def e_copy(r, p, origin_r, origin_p):
+    step = nib // EDGE_CHUNKS
+
+    def e_copy(chunk, r, p, origin_r, origin_p):
         return copy(
-            5, es.at[:, pl.ds(al((r * nc + p) * rows_each, rows_each), rows_each), :],
-            er.at[:, pl.ds(al((origin_p * nr + origin_r) * rows_each, rows_each), rows_each), :],
+            5 + chunk,
+            es.at[pl.ds(chunk * step, step), pl.ds(al((r * nc + p) * rows_each, rows_each), rows_each), :],
+            er.at[
+                pl.ds(chunk * step, step),
+                pl.ds(al((origin_p * nr + origin_r) * rows_each, rows_each), rows_each), :,
+            ],
             r * nc + p, origin_r * nc + origin_p, r, p,
         )
 
-    @pl.loop(1, nd)
-    def _(k):
-        t = lax.rem(me + k, nd)
-        e_copy(t // nc, lax.rem(t, nc), r_me, p_me).start()
+    def e_send(chunk):
+        @pl.loop(1, nd)
+        def _(k):
+            t = lax.rem(me + k, nd)
+            e_copy(chunk, t // nc, lax.rem(t, nc), r_me, p_me).start()
+
+    for chunk in range(EDGE_CHUNKS):
+        begin, end = chunk * step * 128, (chunk + 1) * step * 128
+        for i in range(begin // cb, end // cb):
+            outer = dot_split(right, split(tsc[i].reshape(ow * seq, cz)))
+            count = jnp.sum(mask_right * mask_left[i : i + 1, :], axis=1, keepdims=True)
+            p1[i * cb : (i + 1) * cb, :] = pair_ref[i] + outer / (1.0 + count)
+        part = split(layer_norm(p1[begin:end, :]))
+        raw = dot_split(w_edges, part, NT)
+        edge = sigmoid(raw[: 2 * tri]) * raw[2 * tri :]
+        edge = edge * valid[:, begin:end]
+        for b in range(step):
+            es[chunk * step + b] = edge[:, b * 128 : (b + 1) * 128]
+        e_send(chunk)
 
     er[:, pl.ds(al((p_me * nr + r_me) * rows_each, rows_each), rows_each), :] = es[
         :, pl.ds(al(me * rows_each, rows_each), rows_each), :
@@ -479,12 +503,41 @@
     loads[11].wait()
     loads[12].wait()
     loads[13].wait()
-    out_gate = sigmoid(dot_split(tri_split, split(tgate_ref[...])))
+    pair_one = p1[...]
+    out_gate = sigmoid(dot_split(split(layer_norm(pair_one)), split(tgate_ref[...])))
+    w_out = split(tout_ref[...])
+    w_in = split(xin_ref[...])
+    w_back = split(xout_ref[...])
+
+    @pl.loop(1, nr)
+    def _(k):
+        r = lax.rem(r_me + k, nr)
+        q_copy(r, r_me).wait_send()
+        m_copy(r, r_me).wait_send()
+
+    @pl.loop(0, nr)
+    def _(k):
+        r = lax.rem(r_me + k, nr)
+
+        @pl.when(jnp.logical_or(r != r_me, home != p_me))
+        def _():
+            fr_copy(r, home, r_me, p_me).wait_send()
+
+    for k in range(1, nc):
+        fl_copy(lax.rem(p_me + k, nc), p_me).wait_send()
 
     @pl.loop(1, nd)
     def _(k):
         t = lax.rem(me + k, nd)
-        e_copy(r_me, p_me, t // nc, lax.rem(t, nc)).wait_recv()
+        b_copy(t // nc, lax.rem(t, nc), r_me, p_me).wait_send()
+        for chunk in range(EDGE_CHUNKS):
+            e_copy(chunk, t // nc, lax.rem(t, nc), r_me, p_me).wait_send()
+
+    @pl.loop(1, nd)
+    def _(k):
+        t = lax.rem(me + k, nd)
+        for chunk in range(EDGE_CHUNKS):
+            e_copy(chunk, r_me, p_me, t // nc, lax.rem(t, nc)).wait_recv()
 
     def edge_blocks(row):
         blocks = []
@@ -495,6 +548,22 @@
                     jnp.concatenate([half[:, n * cb : (n + 1) * cb] for half in halves], axis=1)
                 )
         return blocks
+
+    some = crows // CROSS_CHUNKS
+
+    def c_copy(chunk, r, p, origin):
+        return copy(
+            5 + EDGE_CHUNKS + chunk,
+            cs.at[p, pl.ds(al(r * crows + chunk * some, some), some), :],
+            cr.at[pl.ds(al(origin * crows + chunk * some, some), some), :],
+            r * nc + p, origin, r, p,
+        )
+
+    def c_send(chunk):
+        @pl.loop(1, nd)
+        def _(k):
+            t = lax.rem(me + k, nd)
+            c_copy(chunk, t // nc, lax.rem(t, nc), me).start()
 
     for c in range(cpd):
         blocks = edge_blocks(c)
@@ -508,59 +577,26 @@
             )
             for b in range(nib):
                 cs[p, pl.ds(c * nib + b, nr, stride=crows), :] = packed[b * nr : (b + 1) * nr]
-
-    def c_copy(r, p, origin):
-        return copy(
-            6, cs.at[p, pl.ds(al(r * crows, crows), crows), :],
-            cr.at[pl.ds(al(origin * crows, crows), crows), :],
-            r * nc + p, origin, r, p,
-        )
+        if (c + 1) % (cpd // CROSS_CHUNKS) == 0:
+            c_send(c // (cpd // CROSS_CHUNKS))
+
+    cr[pl.ds(al(me * crows, crows), crows), :] = cs[p_me, pl.ds(al(r_me * crows, crows), crows), :]
 
     @pl.loop(1, nd)
     def _(k):
         t = lax.rem(me + k, nd)
-        c_copy(t // nc, lax.rem(t, nc), me).start()
-
-    cr[pl.ds(al(me * crows, crows), crows), :] = cs[p_me, pl.ds(al(r_me * crows, crows), crows), :]
-
-    @pl.loop(1, nd)
-    def _(k):
-        t = lax.rem(me + k, nd)
-        c_copy(r_me, p_me, t).wait_recv()
-
-    w_out = split(tout_ref[...])
+        for chunk in range(CROSS_CHUNKS):
+            c_copy(chunk, t // nc, lax.rem(t, nc), me).wait_send()
+            c_copy(chunk, r_me, p_me, t).wait_recv()
+
     tri_rows = []
     for b in range(nib):
         channels = cr[pl.ds(b, tri, stride=nib), :]
         tri_rows.append(dot_split(split(layer_norm(channels.T)), w_out))
     triangle = jnp.concatenate(tri_rows, axis=0) * out_gate
     pair_mid = pair_one + triangle
-    hidden = jnp.maximum(mm(layer_norm(pair_mid), xin_ref[...]), 0.0)
-    npair_ref[...] = (pair_mid + mm(hidden, xout_ref[...])).reshape(rb, cb, cz)
-
-    @pl.loop(1, nr)
-    def _(k):
-        r = lax.rem(r_me + k, nr)
-        q_copy(r, r_me).wait_send()
-        m_copy(r, r_me).wait_send()
-
-    @pl.loop(0, nr)
-    def _(k):
-        r = lax.rem(r_me + k, nr)
-
-        @pl.when(jnp.logical_or(r != r_me, home != p_me))
-        def _():
-            fr_copy(r, home, r_me, p_me).wait_send()
-
-    for k in range(1, nc):
-        fl_copy(lax.rem(p_me + k, nc), p_me).wait_send()
-
-    @pl.loop(1, nd)
-    def _(k):
-        t = lax.rem(me + k, nd)
-        b_copy(t // nc, lax.rem(t, nc), r_me, p_me).wait_send()
-        e_copy(t // nc, lax.rem(t, nc), r_me, p_me).wait_send()
-        c_copy(t // nc, lax.rem(t, nc), me).wait_send()
+    hidden = jnp.maximum(dot_split(split(layer_norm(pair_mid)), w_in), 0.0)
+    npair_ref[...] = (pair_mid + dot_split(split(hidden), w_back)).reshape(rb, cb, cz)
 
 
 def fused(sizes, *args):
@@ -624,7 +660,8 @@
         out_specs=(vmem, vmem),
         scratch_shapes=[pltpu.VMEM(m.shape, m.dtype) for m in operands]
         + [pltpu.VMEM(s, f32) for s in scratch]
-        + [pltpu.SemaphoreType.DMA((7, nd)), pltpu.SemaphoreType.DMA((7, nd))]
+        + [pltpu.VMEM((ow, 3 * ow, cz), jnp.bfloat16)]
+        + [pltpu.SemaphoreType.DMA((5 + EDGE_CHUNKS + CROSS_CHUNKS, nd))] * 2
         + [pltpu.SemaphoreType.DMA((len(operands),))],
         compiler_params=pltpu.CompilerParams(
             collective_id=0, has_side_effects=True, vmem_limit_bytes=63 * 1024 * 1024
@@ -648,7 +685,8 @@
         and (heads // (nr // sb)) * depth * 4 % 128 == 0 and sb * (oin.shape[1] // 2) % 128 == 0
         and rb % (128 // cb) == 0 and (heads // (nr // sb)) * depth * 2 == 128
         and (heads // (nr // sb)) * (rb * cb // 128) % 8 == 0
-        and tout.shape[0] // (nr * nc) * (rb * cb // 128) % 8 == 0
+        and tout.shape[0] // (nr * nc) * (rb * cb // 128) % (8 * CROSS_CHUNKS) == 0
+        and (rb * cb // 128) % EDGE_CHUNKS == 0 and tout.shape[0] // (nr * nc) % CROSS_CHUNKS == 0
     )
 
 

time: 60.1 us -> 58.8 us (0.978)
  Pallas kernels: 56.2 us -> 54.9 us
    pallas_call x1, Pallas kernels: 56.2 us -> 54.9 us  [fused(): pl.pallas_call(functools.partial(block_kernel, sizes, len(operands)), out...]
where the time goes in v3:
time: 58.8 us; the launch traced here: 58.6 us
  Pallas kernels  54.9 us (93%)
  local copies, waits for them, and re-layouts  3.05 us (5%)
  between operations  0.64 us (1%)
    pallas_call x1, Pallas kernels, fused(): pl.pallas_call(functools.partial(block_kernel, sizes, len(operands)), out...  54.9 us
    unnamed x2, local copies, waits for them, and re-layouts  3.05 us

profile of v3, /device:TPU:0, one launch (start us, length us, event | category | flops | bytes accessed | tf_op | source)
XLA Modules:
  0.0 58.6 jit_solution(11737219655253004455)
XLA Ops:
  0.6 54.9 %shard_map.194 = (f32[4,8,256]{2,1,0:T(8,128)}, f32[8,64,128]{2,1,0:T(8,128)}) custom-call(f32[8,64,128]{2,1,0:T(8,128)} %refs_0_.1, f32[4,8,256]{2,1,0:T(8,128)} %refs_1_.1, s32[1,128]{1,0:T(1,128)} %bitcast.5, s32[4,8]{1,0:T(4,128)} %refs_3_.1, f32[256,1024]{1,0:T(8,128)} %refs_4_.1, f32[8,128]{1,0:T(8,128)} %bitcast.4, f32[256,256]{1,0:T(8,128)} %refs_6_.1, ...), custom_call_target="tpu_custom_call" | custom-call | tf_op jit(solution)/shard_map/pallas_call | solution.py:653
  55.6 1.4 %copy.23 = f32[4,8,256]{2,1,0:T(8,128)} copy(f32[4,8,256]{2,1,0:T(8,128)} %get-tuple-element.4) | data formatting | bytes 65536
  56.9 1.7 %copy.24 = f32[8,64,128]{2,1,0:T(8,128)} copy(f32[8,64,128]{2,1,0:T(8,128)} %get-tuple-element.5) | data formatting | bytes 524288
